TPU v7x, 512 devices: a whole 4x4x16 slice. The times are simulated.
512 devices in a mesh: fsdp: 8 (over x, core), ctx: 64 (over z, y).
Axes of the slice: x: 4, y: 4, z: 16, core: 2. Of those that a mesh axis runs over, the one named last changes fastest.
Arguments:
- tokens: bfloat16 [8, 8192, 4096], P('fsdp', 'ctx'), may hold values from -64 to 64
- doc_start: int32 [8, 8192], P('fsdp', 'ctx'), may hold values from 0 to 8191, as said below
- out_grad: bfloat16 [8, 8192, 1024], P('fsdp', 'ctx'), may hold values from -6 to 6
- w_qkv: bfloat16 [4096, 1280], P(('fsdp', 'ctx')), may hold values from -1 to 1
Outputs:
- grad_tokens: bfloat16 [8, 8192, 4096], P('fsdp', 'ctx')
Inputs may be any that keep to these rules, and one draw needn't show every extreme that they name: Documents are runs of consecutive tokens of 1 to 385 tokens; doc_start gives each token the position in its sequence of its document's first token, and every sequence holds a document of exactly 385 tokens.
All inputs are finite; a program needn't handle non-finite values.
Results may differ from a plain program's by a relative error of at most 0.04.
Values may be sent and summed in bfloat16 or wider, within the bound.
No kernel may reach another device: no remote copies, remote signals or barrier semaphores. Data moves between devices by JAX's collectives and lax.ppermute only.
A program may use at most 64 MiB of HBM per device.

v0:
```python
import math
import jax
import jax.numpy as jnp
from jax import lax
from jax.sharding import PartitionSpec as P

HQ = 8
HD = 128
REACH = 4
ROPE_BASE = 500000.0
MASKED = -1e30


def shifted(block, axis, distance):
    devices = range(lax.axis_size(axis))
    route = [(i - distance, i) for i in devices if i - distance in devices]
    return lax.ppermute(block, axis, route)


def angles_for(positions, head_size):
    half_size = head_size // 2
    inverse = jnp.power(
        jnp.float32(ROPE_BASE), -jnp.arange(half_size, dtype=jnp.float32) / half_size
    )
    phase_angle = positions.astype(jnp.float32)[:, None] * inverse[None, :]
    return (jnp.cos(phase_angle), jnp.sin(phase_angle))


def rotate(vectors, cos_part, sin_part):
    half_size = vectors.shape[-1] // 2
    first_half = vectors[..., :half_size]
    second_half = vectors[..., half_size:]
    return jnp.concatenate(
        [
            first_half * cos_part - second_half * sin_part,
            second_half * cos_part + first_half * sin_part,
        ],
        axis=-1,
    )


def unrotate(vectors, cos_part, sin_part):
    half_size = vectors.shape[-1] // 2
    first_half = vectors[..., :half_size]
    second_half = vectors[..., half_size:]
    return jnp.concatenate(
        [
            first_half * cos_part + second_half * sin_part,
            second_half * cos_part - first_half * sin_part,
        ],
        axis=-1,
    )


def allowed_pairs(query_index, begin_rows, key_start, row_count):
    key_index = key_start + jnp.arange(row_count, dtype=jnp.int32)
    return (key_index[None, :] <= query_index[:, None]) & (
        key_index[None, :] >= begin_rows[:, None]
    )


def forward_block(running, query_block, pair_block, allowed, score_scale):
    top_run, total_run, weighted = running
    key_block = pair_block[:, :HD]
    value_block = pair_block[:, HD:]
    scores = (
        jnp.einsum("qhd,kd->hqk", query_block, key_block, preferred_element_type=jnp.float32)
        * score_scale
    )
    scores = jnp.where(allowed[None], scores, MASKED)
    top_new = jnp.maximum(top_run, jnp.max(scores, axis=-1))
    factor = jnp.exp(top_run - top_new)
    unnormed = jnp.where(allowed[None], jnp.exp(scores - top_new[..., None]), 0.0)
    total_new = total_run * factor + jnp.sum(unnormed, axis=-1)
    weighted = weighted * factor[..., None] + jnp.einsum(
        "hqk,kd->hqd", unnormed, value_block.astype(jnp.float32)
    )
    return (top_new, total_new, weighted)


def backward_block(query_block, pair_block, allowed, log_total, grad_block, row_delta, score_scale):
    key_block = pair_block[:, :HD]
    value_block = pair_block[:, HD:]
    scores = (
        jnp.einsum("qhd,kd->hqk", query_block, key_block, preferred_element_type=jnp.float32)
        * score_scale
    )
    probs = jnp.where(allowed[None], jnp.exp(scores - log_total[..., None]), 0.0)
    probs_low = probs.astype(jnp.bfloat16)
    grad_value = jnp.einsum(
        "hqk,qhd->kd", probs_low, grad_block, preferred_element_type=jnp.float32
    )
    grad_probs = jnp.einsum(
        "qhd,kd->hqk", grad_block, value_block, preferred_element_type=jnp.float32
    )
    grad_scores = (probs * (grad_probs - row_delta[..., None])).astype(jnp.bfloat16)
    grad_query = (
        jnp.einsum("hqk,kd->qhd", grad_scores, key_block, preferred_element_type=jnp.float32)
        * score_scale
    )
    grad_key = (
        jnp.einsum("hqk,qhd->kd", grad_scores, query_block, preferred_element_type=jnp.float32)
        * score_scale
    )
    return (grad_query, jnp.concatenate([grad_key, grad_value], axis=1))


def local(tokens, doc_start, out_grad, w_qkv):
    row_count = tokens.shape[1]
    score_scale = 1.0 / math.sqrt(HD)
    panel_all = lax.all_gather(w_qkv, ("fsdp", "ctx"), axis=0, tiled=True)
    features = tokens[0]
    begin_rows = doc_start[0]
    grad_rows = out_grad[0].reshape(row_count, HQ, HD)
    first_row = lax.axis_index("ctx") * row_count
    query_index = first_row + jnp.arange(row_count, dtype=jnp.int32)
    projected = jnp.dot(features, panel_all, preferred_element_type=jnp.float32)
    cos_part, sin_part = angles_for(query_index - begin_rows, HD)
    queries = rotate(
        projected[:, : HQ * HD].reshape(row_count, HQ, HD),
        cos_part[:, None, :],
        sin_part[:, None, :],
    ).astype(jnp.bfloat16)
    own_keys = rotate(projected[:, HQ * HD : HQ * HD + HD], cos_part, sin_part)
    pair_rows = jnp.concatenate([own_keys, projected[:, HQ * HD + HD :]], axis=1).astype(
        jnp.bfloat16
    )
    pair_blocks = [pair_rows]
    moving = pair_rows
    for distance in range(1, REACH):
        moving = shifted(moving, "ctx", 1)
        pair_blocks.append(moving)
    pair_masks = [
        allowed_pairs(query_index, begin_rows, first_row - distance * row_count, row_count)
        for distance in range(REACH)
    ]
    running = (
        jnp.full((HQ, row_count), MASKED, jnp.float32),
        jnp.zeros((HQ, row_count), jnp.float32),
        jnp.zeros((HQ, row_count, HD), jnp.float32),
    )
    for distance in range(REACH):
        pair_block = pair_blocks[distance]
        allowed = pair_masks[distance]
        running = forward_block(running, queries, pair_block, allowed, score_scale)
    top_run, total_run, weighted = running
    log_total = top_run + jnp.log(total_run)
    attn_out = lax.optimization_barrier(
        jnp.transpose(weighted / total_run[..., None], (1, 0, 2)).astype(jnp.bfloat16)
    )
    row_delta = jnp.sum(grad_rows.astype(jnp.float32) * attn_out.astype(jnp.float32), axis=-1).T
    grad_query = jnp.zeros((row_count, HQ, HD), jnp.float32)
    pair_grads = []
    for distance in range(REACH):
        pair_block = pair_blocks[distance]
        allowed = pair_masks[distance]
        step_query, step_pairs = backward_block(
            queries, pair_block, allowed, log_total, grad_rows, row_delta, score_scale
        )
        grad_query = grad_query + step_query
        pair_grads.append(step_pairs)
    pair_total = pair_grads[REACH - 1]
    for distance in range(REACH - 2, -1, -1):
        pair_total = shifted(pair_total, "ctx", -1) + pair_grads[distance]
    grad_q_pre = unrotate(grad_query, cos_part[:, None, :], sin_part[:, None, :]).reshape(
        row_count, HQ * HD
    )
    grad_k_pre = unrotate(pair_total[:, :HD], cos_part, sin_part)
    all_grads = jnp.concatenate(
        [
            grad_q_pre.astype(jnp.bfloat16),
            grad_k_pre.astype(jnp.bfloat16),
            pair_total[:, HD:].astype(jnp.bfloat16),
        ],
        axis=1,
    )
    result = lax.dot_general(
        all_grads, panel_all, (((1,), (1,)), ((), ())), preferred_element_type=jnp.float32
    )
    return result.astype(jnp.bfloat16)[None]


def solution(mesh):
    placed = (
        P("fsdp", "ctx", None),
        P("fsdp", "ctx"),
        P("fsdp", "ctx", None),
        P(("fsdp", "ctx"), None),
    )
    return jax.shard_map(
        local, mesh=mesh, in_specs=placed, out_specs=P("fsdp", "ctx", None), check_vma=False
    )
```

profile of v0, /device:TPU:120, one launch (start us, length us, event | category | flops | bytes accessed | tf_op | source)
XLA Modules:
  0.0 319.3 jit_solution(14078913883701712490)
XLA Ops:
  7.3 1.1 copy.104
  8.4 0.9 copy.106
  9.9 1.4 compare_and_fusion.3
  11.3 217.0 %all-gather.2.cloned.1.call-done = bf16[4096,1280]{1,0:T(8,128)(2,1)} async-done(((bf16[8,1280]{1,0:T(8,128)(2,1)}), bf16[4096,1280]{1,0:T(8,128)(2,1)}) %all-gather.2.cloned.1.call-update) | async-done | bytes 10485776 | tf_op jit(solution)/shard_map/all_gather | solution.py:111
  228.3 5.5 %fusion.32 = f32[128,1280]{1,0:T(8,128)S(1)} fusion(bf16[4096,1280]{1,0:T(8,128)(2,1)} %all-gather.2.cloned.1.call-done, bf16[1,128,4096]{2,1,0:T(8,128)(2,1)S(1)} %copy-done), kind=kOutput, calls=%fused_computation.56 | convolution fusion | flops 1342177280 | bytes 12189696 | tf_op jit(solution)/shard_map/dot_general | solution.py:117
  235.2 2.6 collective-permute-start
  238.5 2.9 collective-permute-done
  241.4 5.9 %collective-permute-start.1 = (bf16[128,256]{1,0:T(8,128)(2,1)S(1)}, bf16[128,256]{1,0:T(8,128)(2,1)S(1)}, u32[]{:S(2)}, u32[]{:S(2)}) collective-permute-start(bf16[128,256]{1,0:T(8,128)(2,1)S(1)} %collective-permute-done), channel_id=1, source_target_pairs={{0,1},{1,2},{2,3},{3,4},{4,5},{5,6},{6,7},{7,8},{8,9},{9,10},{10,1... | collective-permute-start | bytes 196616 | tf_op jit(solution)/shard_map/ppermute | solution.py:17
  247.6 1.6 collective-permute-done.1
  249.2 7.6 %collective-permute-start.2 = (bf16[128,256]{1,0:T(8,128)(2,1)S(1)}, bf16[128,256]{1,0:T(8,128)(2,1)S(1)}, u32[]{:S(2)}, u32[]{:S(2)}) collective-permute-start(bf16[128,256]{1,0:T(8,128)(2,1)S(1)} %collective-permute-done.1), channel_id=1, source_target_pairs={{0,1},{1,2},{2,3},{3,4},{4,5},{5,6},{6,7},{7,8},{8,9},{9,10},{10,1... | collective-permute-start | bytes 196616 | tf_op jit(solution)/shard_map/ppermute | solution.py:17
  256.8 1.0 select_reduce_fusion.1
  257.8 0.8 collective-permute-done.2
  258.7 1.0 select_reduce_fusion
  261.3 0.8 fusion.39
  262.4 1.0 convolution_bitcast_fusion.14
  263.8 1.1 fusion.12
  264.9 1.1 fusion.14
  265.9 1.1 fusion.27
  267.0 1.2 multiply_reduce_fusion
  269.0 1.0 fusion.23
  270.9 1.9 collective-permute-start.3
  273.1 0.9 fusion.30
  276.0 1.0 convolution_bitcast_fusion.12
  277.0 4.8 %collective-permute-done.3 = f32[128,256]{0,1:T(8,128)} collective-permute-done((f32[128,256]{0,1:T(8,128)}, f32[128,256]{0,1:T(8,128)}, u32[]{:S(2)}, u32[]{:S(2)}) %collective-permute-start.3) | collective-permute-done | bytes 131104 | tf_op jit(solution)/shard_map/ppermute | solution.py:17
  281.8 0.9 maximum_add_fusion
  282.7 1.9 collective-permute-start.4
  284.6 1.0 convolution_bitcast_fusion.10
  285.6 7.3 %collective-permute-done.4 = f32[128,256]{0,1:T(8,128)S(1)} collective-permute-done((f32[128,256]{0,1:T(8,128)S(1)}, f32[128,256]{0,1:T(8,128)S(1)}, u32[]{:S(2)}, u32[]{:S(2)}) %collective-permute-start.4) | collective-permute-done | bytes 131104 | tf_op jit(solution)/shard_map/ppermute | solution.py:17
  292.9 2.1 collective-permute-start.5
  295.0 0.9 convolution_bitcast_fusion.8
  295.9 7.1 %collective-permute-done.5 = f32[128,256]{0,1:T(8,128)S(1)} collective-permute-done((f32[128,256]{0,1:T(8,128)S(1)}, f32[128,256]{0,1:T(8,128)S(1)}, u32[]{:S(2)}, u32[]{:S(2)}) %collective-permute-start.5) | collective-permute-done | bytes 131104 | tf_op jit(solution)/shard_map/ppermute | solution.py:17
  303.9 8.5 %fusion = bf16[1,128,4096]{2,1,0:T(8,128)(2,1)} fusion(bf16[4096,1280]{1,0:T(8,128)(2,1)} %all-gather.2.cloned.1.call-done, bf16[128,128]{0,1:T(8,128)(2,1)S(1)} %slice.133, bf16[128,64]{0,1:T(8,128)(2,1)S(1)} %get-tuple-element.20, bf16[128,64]{0,1:T(8,128)(2,1)S(1)} %get-tuple-element.19, bf16[128,1024]{0,1:T(8,128)(2,1)S(1)} %bitcast.251), kind=kOutput, calls=%fused_computation.1 | convolution fusion | flops 1344012288 | bytes 11862016 | tf_op jit(solution)/shard_map/dot_general | solution.py:177
  (78 shorter events, 10.7 us)
Async XLA Ops:
  6.5 221.8 %copy-start = (bf16[1,128,4096]{2,1,0:T(8,128)(2,1)S(1)}, bf16[1,128,4096]{2,1,0:T(8,128)(2,1)}, u32[]{:S(2)}) copy-start(bf16[1,128,4096]{2,1,0:T(8,128)(2,1)} %param.4) | copy-start | bytes 3145732
  6.5 221.8 %all-gather.2.cloned.1.call-start = ((), (), s32[]{:S(2)}) async-start(), calls=%async_computation | async-start | bytes 10506240 | tf_op jit(solution)/shard_map/all_gather | solution.py:111
  9.3 225.2 %copy-start.14 = (f32[64]{0:T(128)}, f32[64]{0:T(128)S(1)}, u32[]{:S(2)}) copy-start(f32[64]{0:T(128)S(1)} %multiply_power_fusion) | copy-start | bytes 772
  9.9 224.5 %copy-start.13 = (f32[128]{0:T(128)}, f32[128]{0:T(128)S(1)}, u32[]{:S(2)}) copy-start(f32[128]{0:T(128)S(1)} %get-tuple-element.40) | copy-start | bytes 1540
  11.3 236.0 %copy-start.1 = (pred[128,128]{0,1:T(8,128)(4,1)}, pred[128,128]{0,1:T(8,128)(4,1)S(1)}, u32[]{:S(2)}) copy-start(pred[128,128]{0,1:T(8,128)(4,1)S(1)} %get-tuple-element.29) | copy-start | bytes 49156
  234.7 22.1 %copy-start.9 = (bf16[128,64]{0,1:T(8,128)(2,1)}, bf16[128,64]{0,1:T(8,128)(2,1)S(1)}, u32[]{:S(2)}) copy-start(bf16[128,64]{0,1:T(8,128)(2,1)S(1)} %get-tuple-element.21) | copy-start | bytes 49156
  234.7 22.1 %copy-start.11 = (bf16[128,64]{0,1:T(8,128)(2,1)}, bf16[128,64]{0,1:T(8,128)(2,1)S(1)}, u32[]{:S(2)}) copy-start(bf16[128,64]{0,1:T(8,128)(2,1)S(1)} %get-tuple-element.22) | copy-start | bytes 49156
  234.8 22.0 %copy-start.4 = (f32[128,64]{1,0:T(8,128)}, f32[128,64]{1,0:T(8,128)S(1)}, u32[]{:S(2)}) copy-start(f32[128,64]{1,0:T(8,128)S(1)} %copy.100) | copy-start | bytes 98308
  234.9 21.9 %copy-start.6 = (f32[128,64]{1,0:T(8,128)}, f32[128,64]{1,0:T(8,128)S(1)}, u32[]{:S(2)}) copy-start(f32[128,64]{1,0:T(8,128)S(1)} %copy.98) | copy-start | bytes 98308
  235.2 6.2 %collective-permute-start = (bf16[128,256]{1,0:T(8,128)(2,1)S(1)}, bf16[128,256]{1,0:T(8,128)(2,1)S(1)}, u32[]{:S(2)}, u32[]{:S(2)}) collective-permute-start(bf16[128,256]{1,0:T(8,128)(2,1)S(1)} %pad_maximum_fusion.3), channel_id=1, source_target_pairs={{0,1},{1,2},{2,3},{3,4},{4,5},{5,6},{6,7},{7,8},{8,9},{9,10},{10,1... | collective-permute-start | bytes 196616 | tf_op jit(solution)/shard_map/ppermute | solution.py:17
  237.8 35.0 %copy-start.3 = (pred[128,128]{0,1:T(8,128)(4,1)S(1)}, pred[128,128]{0,1:T(8,128)(4,1)}, u32[]{:S(2)}) copy-start(pred[128,128]{0,1:T(8,128)(4,1)} %get-tuple-element.27) | copy-start | bytes 49156
  241.4 7.8 %collective-permute-start.1 = (bf16[128,256]{1,0:T(8,128)(2,1)S(1)}, bf16[128,256]{1,0:T(8,128)(2,1)S(1)}, u32[]{:S(2)}, u32[]{:S(2)}) collective-permute-start(bf16[128,256]{1,0:T(8,128)(2,1)S(1)} %collective-permute-done), channel_id=1, source_target_pairs={{0,1},{1,2},{2,3},{3,4},{4,5},{5,6},{6,7},{7,8},{8,9},{9,10},{10,1... | collective-permute-start | bytes 196616 | tf_op jit(solution)/shard_map/ppermute | solution.py:17
  247.6 26.4 %copy-start.2 = (pred[128,128]{0,1:T(8,128)(4,1)S(1)}, pred[128,128]{0,1:T(8,128)(4,1)}, u32[]{:S(2)}) copy-start(pred[128,128]{0,1:T(8,128)(4,1)} %copy-done.1) | copy-start | bytes 49156
  249.2 9.5 %collective-permute-start.2 = (bf16[128,256]{1,0:T(8,128)(2,1)S(1)}, bf16[128,256]{1,0:T(8,128)(2,1)S(1)}, u32[]{:S(2)}, u32[]{:S(2)}) collective-permute-start(bf16[128,256]{1,0:T(8,128)(2,1)S(1)} %collective-permute-done.1), channel_id=1, source_target_pairs={{0,1},{1,2},{2,3},{3,4},{4,5},{5,6},{6,7},{7,8},{8,9},{9,10},{10,1... | collective-permute-start | bytes 196616 | tf_op jit(solution)/shard_map/ppermute | solution.py:17
  256.8 11.9 %copy-start.10 = (bf16[128,64]{0,1:T(8,128)(2,1)S(1)}, bf16[128,64]{0,1:T(8,128)(2,1)}, u32[]{:S(2)}) copy-start(bf16[128,64]{0,1:T(8,128)(2,1)} %copy-done.9) | copy-start | bytes 49156
  256.8 11.9 %copy-start.12 = (bf16[128,64]{0,1:T(8,128)(2,1)S(1)}, bf16[128,64]{0,1:T(8,128)(2,1)}, u32[]{:S(2)}) copy-start(bf16[128,64]{0,1:T(8,128)(2,1)} %copy-done.11) | copy-start | bytes 49156
  262.2 13.2 %copy-start.5 = (f32[128,64]{1,0:T(8,128)S(1)}, f32[128,64]{1,0:T(8,128)}, u32[]{:S(2)}) copy-start(f32[128,64]{1,0:T(8,128)} %copy-done.4) | copy-start | bytes 98308
  262.2 13.2 %copy-start.7 = (f32[128,64]{1,0:T(8,128)S(1)}, f32[128,64]{1,0:T(8,128)}, u32[]{:S(2)}) copy-start(f32[128,64]{1,0:T(8,128)} %copy-done.6) | copy-start | bytes 98308
  262.3 11.9 %copy-start.8 = (f32[8,128]{1,0:T(8,128)}, f32[8,128]{1,0:T(8,128)S(1)}, u32[]{:S(2)}) copy-start(f32[8,128]{1,0:T(8,128)S(1)} %log_add_fusion) | copy-start | bytes 12292
  270.9 10.8 %collective-permute-start.3 = (f32[128,256]{0,1:T(8,128)}, f32[128,256]{0,1:T(8,128)}, u32[]{:S(2)}, u32[]{:S(2)}) collective-permute-start(f32[128,256]{0,1:T(8,128)} %pad_maximum_fusion.2), channel_id=1, source_target_pairs={{1,0},{2,1},{3,2},{4,3},{5,4},{6,5},{7,6},{8,7},{9,8},{10,9},{11,1... | collective-permute-start | bytes 393224 | tf_op jit(solution)/shard_map/ppermute | solution.py:17
  282.7 10.2 %collective-permute-start.4 = (f32[128,256]{0,1:T(8,128)S(1)}, f32[128,256]{0,1:T(8,128)S(1)}, u32[]{:S(2)}, u32[]{:S(2)}) collective-permute-start(f32[128,256]{0,1:T(8,128)S(1)} %maximum_add_fusion), channel_id=1, source_target_pairs={{1,0},{2,1},{3,2},{4,3},{5,4},{6,5},{7,6},{8,7},{9,8},{10,9},{11,1... | collective-permute-start | bytes 393224 | tf_op jit(solution)/shard_map/ppermute | solution.py:17
  292.9 10.2 %collective-permute-start.5 = (f32[128,256]{0,1:T(8,128)S(1)}, f32[128,256]{0,1:T(8,128)S(1)}, u32[]{:S(2)}, u32[]{:S(2)}) collective-permute-start(f32[128,256]{0,1:T(8,128)S(1)} %maximum_add_fusion.1), channel_id=1, source_target_pairs={{1,0},{2,1},{3,2},{4,3},{5,4},{6,5},{7,6},{8,7},{9,8},{10,9},{11,1... | collective-permute-start | bytes 393224 | tf_op jit(solution)/shard_map/ppermute | solution.py:17
Sparse Core Ops, SparseCore 0:
  12.0 216.2 all-gather.1
where the time goes:
time: 321 us; the launch traced here: 319 us
  waiting for transfers between devices  242 us (75%)
  matrix products  28.4 us (9%)
  starting transfers between devices  22 us (7%)
  between operations  14 us (4%)
  other arithmetic  9.45 us (3%)
  local copies, waits for them, and re-layouts  3.22 us (1%)
    all_gather x1, waiting for transfers between devices, local(): panel_all = lax.all_gather(w_qkv, ('fsdp', 'ctx'), axis=0, tiled=True)  217 us
    ppermute x6, waiting for transfers between devices, shifted(): return lax.ppermute(block, axis, route)  24.6 us
    ppermute x6, starting transfers between devices, shifted(): return lax.ppermute(block, axis, route)  22 us
    dot_general x1, matrix products, local(): lax.dot_general(all_grads, panel_all, (((1,), (1,)), ((), ())), preferred...  8.48 us
  transfers between devices with their start and end apart: 7, of which 7 were waited for; matrix products, arithmetic and copies ran while one was open for 4% of the time, Pallas kernels for 0%

commit v1 on v0

--- a/solution.py
+++ b/solution.py
@@ -108,7 +108,10 @@
 def local(tokens, doc_start, out_grad, w_qkv):
     row_count = tokens.shape[1]
     score_scale = 1.0 / math.sqrt(HD)
-    panel_all = lax.all_gather(w_qkv, ("fsdp", "ctx"), axis=0, tiled=True)
+    panel_all = jnp.concatenate(
+        lax.all_to_all(jnp.stack([w_qkv] * lax.axis_size(("fsdp", "ctx"))), ("fsdp", "ctx"), 0, 0),
+        axis=0,
+    )
     features = tokens[0]
     begin_rows = doc_start[0]
     grad_rows = out_grad[0].reshape(row_count, HQ, HD)

time: 321 us -> 574 us (1.79)
  waiting for transfers between devices: 242 us -> 482 us
  starting transfers between devices: 22 us -> 45 us
  between operations: 14 us -> 0.62 us
    all_to_all x0 -> x1, waiting for transfers between devices: none -> 454 us  [local(): lax.all_to_all(jnp.stack([w_qkv] * lax.axis_size(('fsdp', 'ctx'))), ('fsd...]
    all_gather x1 -> x0, waiting for transfers between devices: 217 us -> none  [local(): panel_all = lax.all_gather(w_qkv, ('fsdp', 'ctx'), axis=0, tiled=True)]
    all_to_all x0 -> x1, starting transfers between devices: none -> 24.3 us  [local(): lax.all_to_all(jnp.stack([w_qkv] * lax.axis_size(('fsdp', 'ctx'))), ('fsd...]
  transfers between devices with their start and end apart: 7 -> 7, of which waited for: 7 -> 7; matrix products, arithmetic and copies ran while one was open for 4% -> 1% of each run, Pallas kernels for 0% -> 0%
where the time goes in v1:
time: 574 us; the launch traced here: 572 us
  waiting for transfers between devices  482 us (84%)
  starting transfers between devices  45 us (8%)
  matrix products  29 us (5%)
  other arithmetic  8.38 us (1%)
  local copies, waits for them, and re-layouts  7.6 us (1%)
    all_to_all x1, waiting for transfers between devices, local(): lax.all_to_all(jnp.stack([w_qkv] * lax.axis_size(('fsdp', 'ctx'))), ('fsd...  454 us
    ppermute x6, waiting for transfers between devices, shifted(): return lax.ppermute(block, axis, route)  28.1 us
    all_to_all x1, starting transfers between devices, local(): lax.all_to_all(jnp.stack([w_qkv] * lax.axis_size(('fsdp', 'ctx'))), ('fsd...  24.3 us
    ppermute x6, starting transfers between devices, shifted(): return lax.ppermute(block, axis, route)  20.7 us
  transfers between devices with their start and end apart: 7, of which 7 were waited for; matrix products, arithmetic and copies ran while one was open for 1% of the time, Pallas kernels for 0%

profile of v1, /device:TPU:120, one launch (start us, length us, event | category | flops | bytes accessed | tf_op | source)
XLA Modules:
  0.0 572.2 jit_solution(4128652791168895890)
XLA Ops:
  0.0 5.3 stack.2
  5.3 24.3 %all-to-all-start = ((bf16[512,8,1280]{2,1,0:T(8,128)(2,1)}), bf16[512,8,1280]{2,1,0:T(8,128)(2,1)}, u32[]{:S(2)}, u32[]{:S(2)}) async-start(bf16[512,8,1280]{2,1,0:T(8,128)(2,1)} %stack.2), calls=%async_computation | async-start | bytes 20971520 | tf_op jit(solution)/shard_map/all_to_all | solution.py:112
  31.5 453.5 %all-to-all-done = bf16[512,8,1280]{2,1,0:T(8,128)(2,1)} async-done(((bf16[512,8,1280]{2,1,0:T(8,128)(2,1)}), bf16[512,8,1280]{2,1,0:T(8,128)(2,1)}, u32[]{:S(2)}, u32[]{:S(2)}) %all-to-all-start) | async-done | bytes 10485792 | tf_op jit(solution)/shard_map/all_to_all | solution.py:112
  485.0 5.5 fusion.2
  492.0 1.9 collective-permute-start
  494.6 3.6 collective-permute-done
  498.2 5.2 collective-permute-start.1
  503.6 1.6 collective-permute-done.1
  505.3 7.8 %collective-permute-start.2 = (bf16[128,256]{1,0:T(8,128)(2,1)S(1)}, bf16[128,256]{1,0:T(8,128)(2,1)S(1)}, u32[]{:S(2)}, u32[]{:S(2)}) collective-permute-start(bf16[128,256]{1,0:T(8,128)(2,1)S(1)} %collective-permute-done.1), channel_id=1, source_target_pairs={{0,1},{1,2},{2,3},{3,4},{4,5},{5,6},{6,7},{7,8},{8,9},{9,10},{10,1... | collective-permute-start | bytes 196616 | tf_op jit(solution)/shard_map/ppermute | solution.py:17
  513.1 1.0 select_reduce_fusion.1
  514.7 1.0 select_reduce_fusion
  517.6 0.9 fusion.49
  519.0 1.1 fusion.21
  520.0 1.1 fusion.23
  521.1 1.1 fusion.36
  522.2 1.2 multiply_reduce_fusion
  524.2 1.6 convolution_bitcast_fusion.14
  526.5 0.9 fusion.39
  527.7 0.9 fusion.40
  530.1 0.9 pad_maximum_fusion.2
  531.0 1.9 collective-permute-start.3
  532.9 1.0 convolution_bitcast_fusion.12
  533.9 7.6 %collective-permute-done.3 = f32[128,256]{0,1:T(8,128)S(1)} collective-permute-done((f32[128,256]{0,1:T(8,128)S(1)}, f32[128,256]{0,1:T(8,128)S(1)}, u32[]{:S(2)}, u32[]{:S(2)}) %collective-permute-start.3) | collective-permute-done | bytes 131104 | tf_op jit(solution)/shard_map/ppermute | solution.py:17
  541.5 0.9 maximum_add_fusion
  542.4 1.9 collective-permute-start.4
  544.3 1.0 convolution_bitcast_fusion.10
  545.3 7.3 %collective-permute-done.4 = f32[128,256]{0,1:T(8,128)S(1)} collective-permute-done((f32[128,256]{0,1:T(8,128)S(1)}, f32[128,256]{0,1:T(8,128)S(1)}, u32[]{:S(2)}, u32[]{:S(2)}) %collective-permute-start.4) | collective-permute-done | bytes 131104 | tf_op jit(solution)/shard_map/ppermute | solution.py:17
  552.6 1.9 collective-permute-start.5
  554.5 0.9 convolution_bitcast_fusion.8
  555.4 7.3 %collective-permute-done.5 = f32[128,256]{0,1:T(8,128)S(1)} collective-permute-done((f32[128,256]{0,1:T(8,128)S(1)}, f32[128,256]{0,1:T(8,128)S(1)}, u32[]{:S(2)}, u32[]{:S(2)}) %collective-permute-start.5) | collective-permute-done | bytes 131104 | tf_op jit(solution)/shard_map/ppermute | solution.py:17
  562.8 0.9 fusion.102
  563.7 8.5 %fusion.7 = bf16[1,128,4096]{2,1,0:T(8,128)(2,1)} fusion(bf16[512,8,1280]{2,1,0:T(8,128)(2,1)} %all-to-all-done, bf16[128,128]{0,1:T(8,128)(2,1)S(1)} %slice.133, bf16[128,64]{0,1:T(8,128)(2,1)S(1)} %get-tuple-element.20, bf16[128,64]{0,1:T(8,128)(2,1)S(1)} %get-tuple-element.19, bf16[128,1024]{0,1:T(8,128)(2,1)S(1)} %bitcast.258), kind=kOutput, calls=%fused_computation.5 | convolution fusion | flops 1344012288 | bytes 11862016 | tf_op jit(solution)/shard_map/dot_general | solution.py:180
  (84 shorter events, 10.2 us)
Async XLA Ops:
  0.0 485.0 %copy-start = (bf16[1,128,4096]{2,1,0:T(8,128)(2,1)S(1)}, bf16[1,128,4096]{2,1,0:T(8,128)(2,1)}, u32[]{:S(2)}) copy-start(bf16[1,128,4096]{2,1,0:T(8,128)(2,1)} %param.4) | copy-start | bytes 3145732
  5.3 24.4 %copy-start.14 = (bf16[1,128,1024]{2,1,0:T(8,128)(2,1)S(1)}, bf16[1,128,1024]{2,1,0:T(8,128)(2,1)}, u32[]{:S(2)}) copy-start(bf16[1,128,1024]{2,1,0:T(8,128)(2,1)} %param.6) | copy-start | bytes 786436
  5.3 25.4 %copy-start.17 = (s32[1,128]{1,0:T(1,128)S(1)}, s32[1,128]{1,0:T(1,128)}, u32[]{:S(2)}) copy-start(s32[1,128]{1,0:T(1,128)} %param.5) | copy-start | bytes 1540
  5.3 479.7 %all-to-all-start = ((bf16[512,8,1280]{2,1,0:T(8,128)(2,1)}), bf16[512,8,1280]{2,1,0:T(8,128)(2,1)}, u32[]{:S(2)}, u32[]{:S(2)}) async-start(bf16[512,8,1280]{2,1,0:T(8,128)(2,1)} %stack.2), calls=%async_computation | async-start | bytes 20971520 | tf_op jit(solution)/shard_map/all_to_all | solution.py:112
  30.7 460.7 %copy-start.16 = (f32[64]{0:T(128)}, f32[64]{0:T(128)S(1)}, u32[]{:S(2)}) copy-start(f32[64]{0:T(128)S(1)} %multiply_power_fusion) | copy-start | bytes 772
  30.8 460.6 %copy-start.15 = (f32[128]{0:T(128)}, f32[128]{0:T(128)S(1)}, u32[]{:S(2)}) copy-start(f32[128]{0:T(128)S(1)} %get-tuple-element.40) | copy-start | bytes 1540
  31.5 481.5 %copy-start.1 = (pred[128,128]{0,1:T(8,128)(4,1)}, pred[128,128]{0,1:T(8,128)(4,1)S(1)}, u32[]{:S(2)}) copy-start(pred[128,128]{0,1:T(8,128)(4,1)S(1)} %get-tuple-element.29) | copy-start | bytes 49156
  491.1 22.0 %copy-start.10 = (bf16[128,64]{0,1:T(8,128)(2,1)}, bf16[128,64]{0,1:T(8,128)(2,1)S(1)}, u32[]{:S(2)}) copy-start(bf16[128,64]{0,1:T(8,128)(2,1)S(1)} %get-tuple-element.21) | copy-start | bytes 49156
  491.1 22.0 %copy-start.12 = (bf16[128,64]{0,1:T(8,128)(2,1)}, bf16[128,64]{0,1:T(8,128)(2,1)S(1)}, u32[]{:S(2)}) copy-start(bf16[128,64]{0,1:T(8,128)(2,1)S(1)} %get-tuple-element.22) | copy-start | bytes 49156
  491.2 21.9 %copy-start.4 = (f32[128,64]{1,0:T(8,128)}, f32[128,64]{1,0:T(8,128)S(1)}, u32[]{:S(2)}) copy-start(f32[128,64]{1,0:T(8,128)S(1)} %copy.100) | copy-start | bytes 98308
  491.3 21.8 %copy-start.6 = (f32[128,64]{1,0:T(8,128)}, f32[128,64]{1,0:T(8,128)S(1)}, u32[]{:S(2)}) copy-start(f32[128,64]{1,0:T(8,128)S(1)} %copy.98) | copy-start | bytes 98308
  492.0 6.2 %collective-permute-start = (bf16[128,256]{1,0:T(8,128)(2,1)S(1)}, bf16[128,256]{1,0:T(8,128)(2,1)S(1)}, u32[]{:S(2)}, u32[]{:S(2)}) collective-permute-start(bf16[128,256]{1,0:T(8,128)(2,1)S(1)} %pad_maximum_fusion.3), channel_id=1, source_target_pairs={{0,1},{1,2},{2,3},{3,4},{4,5},{5,6},{6,7},{7,8},{8,9},{9,10},{10,1... | collective-permute-start | bytes 196616 | tf_op jit(solution)/shard_map/ppermute | solution.py:17
  493.9 32.4 %copy-start.3 = (pred[128,128]{0,1:T(8,128)(4,1)S(1)}, pred[128,128]{0,1:T(8,128)(4,1)}, u32[]{:S(2)}) copy-start(pred[128,128]{0,1:T(8,128)(4,1)} %get-tuple-element.27) | copy-start | bytes 49156
  494.1 33.3 %copy-start.8 = (pred[128,128]{0,1:T(8,128)(4,1)S(1)}, pred[128,128]{0,1:T(8,128)(4,1)}, u32[]{:S(2)}) copy-start(pred[128,128]{0,1:T(8,128)(4,1)} %get-tuple-element.28) | copy-start | bytes 49156
  498.2 7.1 %collective-permute-start.1 = (bf16[128,256]{1,0:T(8,128)(2,1)S(1)}, bf16[128,256]{1,0:T(8,128)(2,1)S(1)}, u32[]{:S(2)}, u32[]{:S(2)}) collective-permute-start(bf16[128,256]{1,0:T(8,128)(2,1)S(1)} %collective-permute-done), channel_id=1, source_target_pairs={{0,1},{1,2},{2,3},{3,4},{4,5},{5,6},{6,7},{7,8},{8,9},{9,10},{10,1... | collective-permute-start | bytes 196616 | tf_op jit(solution)/shard_map/ppermute | solution.py:17
  505.3 9.5 %collective-permute-start.2 = (bf16[128,256]{1,0:T(8,128)(2,1)S(1)}, bf16[128,256]{1,0:T(8,128)(2,1)S(1)}, u32[]{:S(2)}, u32[]{:S(2)}) collective-permute-start(bf16[128,256]{1,0:T(8,128)(2,1)S(1)} %collective-permute-done.1), channel_id=1, source_target_pairs={{0,1},{1,2},{2,3},{3,4},{4,5},{5,6},{6,7},{7,8},{8,9},{9,10},{10,1... | collective-permute-start | bytes 196616 | tf_op jit(solution)/shard_map/ppermute | solution.py:17
  513.1 10.5 %copy-start.11 = (bf16[128,64]{0,1:T(8,128)(2,1)S(1)}, bf16[128,64]{0,1:T(8,128)(2,1)}, u32[]{:S(2)}) copy-start(bf16[128,64]{0,1:T(8,128)(2,1)} %copy-done.10) | copy-start | bytes 49156
  513.1 10.5 %copy-start.13 = (bf16[128,64]{0,1:T(8,128)(2,1)S(1)}, bf16[128,64]{0,1:T(8,128)(2,1)}, u32[]{:S(2)}) copy-start(bf16[128,64]{0,1:T(8,128)(2,1)} %copy-done.12) | copy-start | bytes 49156
  513.1 12.7 %copy-start.2 = (pred[128,128]{0,1:T(8,128)(4,1)S(1)}, pred[128,128]{0,1:T(8,128)(4,1)}, u32[]{:S(2)}) copy-start(pred[128,128]{0,1:T(8,128)(4,1)} %copy-done.1) | copy-start | bytes 49156
  517.5 11.9 %copy-start.5 = (f32[128,64]{1,0:T(8,128)S(1)}, f32[128,64]{1,0:T(8,128)}, u32[]{:S(2)}) copy-start(f32[128,64]{1,0:T(8,128)} %copy-done.4) | copy-start | bytes 98308
  517.5 11.9 %copy-start.7 = (f32[128,64]{1,0:T(8,128)S(1)}, f32[128,64]{1,0:T(8,128)}, u32[]{:S(2)}) copy-start(f32[128,64]{1,0:T(8,128)} %copy-done.6) | copy-start | bytes 98308
  518.5 10.7 %copy-start.9 = (f32[8,128]{1,0:T(8,128)}, f32[8,128]{1,0:T(8,128)S(1)}, u32[]{:S(2)}) copy-start(f32[8,128]{1,0:T(8,128)S(1)} %log_add_fusion) | copy-start | bytes 12292
  531.0 10.5 %collective-permute-start.3 = (f32[128,256]{0,1:T(8,128)S(1)}, f32[128,256]{0,1:T(8,128)S(1)}, u32[]{:S(2)}, u32[]{:S(2)}) collective-permute-start(f32[128,256]{0,1:T(8,128)S(1)} %pad_maximum_fusion.2), channel_id=1, source_target_pairs={{1,0},{2,1},{3,2},{4,3},{5,4},{6,5},{7,6},{8,7},{9,8},{10,9},{11,1... | collective-permute-start | bytes 393224 | tf_op jit(solution)/shard_map/ppermute | solution.py:17
  542.4 10.2 %collective-permute-start.4 = (f32[128,256]{0,1:T(8,128)S(1)}, f32[128,256]{0,1:T(8,128)S(1)}, u32[]{:S(2)}, u32[]{:S(2)}) collective-permute-start(f32[128,256]{0,1:T(8,128)S(1)} %maximum_add_fusion), channel_id=1, source_target_pairs={{1,0},{2,1},{3,2},{4,3},{5,4},{6,5},{7,6},{8,7},{9,8},{10,9},{11,1... | collective-permute-start | bytes 393224 | tf_op jit(solution)/shard_map/ppermute | solution.py:17
  552.6 10.2 %collective-permute-start.5 = (f32[128,256]{0,1:T(8,128)S(1)}, f32[128,256]{0,1:T(8,128)S(1)}, u32[]{:S(2)}, u32[]{:S(2)}) collective-permute-start(f32[128,256]{0,1:T(8,128)S(1)} %maximum_add_fusion.1), channel_id=1, source_target_pairs={{1,0},{2,1},{3,2},{4,3},{5,4},{6,5},{7,6},{8,7},{9,8},{10,9},{11,1... | collective-permute-start | bytes 393224 | tf_op jit(solution)/shard_map/ppermute | solution.py:17
